TPU v7x, 32 devices: a whole 2x2x4 slice. The times are simulated.
32 devices in a mesh: spatial: 8 (over z, y), dp: 4 (over x, core).
Axes of the slice: x: 2, y: 2, z: 4, core: 2. Of those that a mesh axis runs over, the one named last changes fastest.
Arguments:
- features: bfloat16 [4, 48, 8, 8, 512], P('dp', 'spatial'), may hold values from -6 to 6
- masks: int32 [4, 48, 512], P('dp', 'spatial'), may hold values 0 or 1
- rulebook: int32 [4, 48, 27], P('dp', 'spatial'), may hold values from 0 to 22, as said below
- send_lists: int32 [4, 8, 8, 2], P('dp', 'spatial'), may hold values from 0 to 6, as said below
- conv_weight: bfloat16 [27, 64, 64], replicated, may hold values from -0.15625 to 0.15625
- down_weight: bfloat16 [8, 64, 128], replicated, may hold values from -0.25 to 0.25
- cotangent: bfloat16 [4, 48, 4, 4, 512], P('dp', 'spatial'), may hold values from -6 to 6
Outputs:
- coarse_out: bfloat16 [4, 48, 4, 4, 512], P('dp', 'spatial')
- grad_features: bfloat16 [4, 48, 8, 8, 512], P('dp', 'spatial')
- grad_conv: float32 [27, 64, 64], replicated
- grad_down: float32 [8, 64, 128], replicated
Inputs may be any that keep to these rules, and one draw needn't show every extreme that they name: `send_lists`: with q = d // 4, device d of spatial is region ((q % 2) (1) + q // 2, (d // 2) % 2, d % 2) of a 2^3 grid without wrap. A device sends 2 distinct bricks to each region sharing a face with it, one brick (slot 0) to each sharing only an edge or a corner, and nothing to itself or to other regions; empty slots hold 6. Entries index the owning device's extended list; entry 13 of a brick is the brick's own local index; entries name only own bricks, filled received slots and 22, and each of these appears in the device's rulebook.
All inputs are finite; a program needn't handle non-finite values. No bound on the sum of `masks` on one device may be relied on, other than what follows from the above.
Results may differ from a plain program's by a relative error of at most 0.0095.
Values may be sent and summed in bfloat16 or wider, within the bound.
A program may use at most 192 MiB of HBM per device.

v0:
```python
import functools

import jax
import jax.numpy as jnp
from jax import lax
from jax.experimental import pallas as pl
from jax.experimental.pallas import tpu as pltpu
from jax.sharding import PartitionSpec as P

F32 = jnp.float32
BF16 = jnp.bfloat16
VMEM_BYTES = 56 * 1024 * 1024


def silu_grad(value):
    sig = jax.nn.sigmoid(value)
    return sig * (1.0 + value * (1.0 - sig))


def first_kernel(chosen, feats, mask, masked, keepx, outgoing):
    count = feats.shape[0]
    slots = outgoing.shape[0]
    vox = lax.broadcasted_iota(jnp.int32, (64, 512), 1)
    row = lax.broadcasted_iota(jnp.int32, (64, 512), 0)
    own_row = (vox // 8) == row
    v_index = lax.broadcasted_iota(jnp.int32, (512, 512), 0)
    l_index = lax.broadcasted_iota(jnp.int32, (512, 512), 1)
    spread = ((v_index % 8) == (l_index // 64)).astype(F32).astype(BF16)
    for b in range(count):
        picked = jnp.where(own_row, mask[b : b + 1, :].astype(F32), 0.0).astype(BF16)
        keep = jnp.dot(picked, spread, preferred_element_type=F32)
        keepx[b] = keep.astype(BF16)
        masked[b] = (feats[b].astype(F32) * keep).astype(BF16)
    masked[count] = jnp.zeros((64, 512), BF16)

    def send(s, carry):
        outgoing[s] = masked[chosen[s]]
        return carry

    lax.fori_loop(0, slots, send, 0)


def main_kernel(
    table, masked, arrived, keepx, weight, down, cot,
    out, own, ret, wgrad,
    ext, gext, lhs, asm, dpad, pre, hid, keep, grad, grad_t, wpair, sems,
):
    count = keepx.shape[0]
    slots = arrived.shape[0]
    total = ext.shape[0]
    half_rows = count * 128
    rows = 2 * half_rows
    lane = lax.broadcasted_iota(jnp.int32, (8, 128), 1)

    fetch_own = pltpu.make_async_copy(masked.at[pl.ds(0, count)], ext.at[pl.ds(0, count)], sems.at[0])
    fetch_rest = pltpu.make_async_copy(arrived, ext.at[pl.ds(count, slots)], sems.at[1])
    fetch_own.start()
    fetch_rest.start()
    ext[total - 1] = jnp.zeros((64, 512), BF16)

    def clear(e, carry):
        gext[e] = jnp.zeros((64, 512), F32)
        return carry

    lax.fori_loop(0, total, clear, 0)

    for tap in range(9):
        taps = weight[tap * 192 : tap * 192 + 192, :].astype(F32)
        zero = jnp.zeros((64, 64), F32)
        left = jnp.concatenate([taps, zero], axis=0)
        right = jnp.concatenate([zero, taps], axis=0)
        wpair[tap * 256 : tap * 256 + 256, :] = jnp.concatenate([left, right], axis=1).astype(BF16)
    fetch_own.wait()
    fetch_rest.wait()

    def gather_brick(b, carry):
        for y_pos in range(3):
            for x_pos in range(3):
                src = ((48, 64), (0, 64), (0, 16))[x_pos]
                cut = ((8, 16), (0, 64), (0, 8))[x_pos]
                dst = ((0, 1), (1, 9), (9, 10))[x_pos]
                tiles = (dst[1] - dst[0], 8, 128)
                low = lax.broadcasted_iota(jnp.int32, tiles, 2) < 64
                base = x_pos * 9 + y_pos * 3

                def load(index, lo):
                    part = ext[index, src[0] : src[1], lo : lo + 128].astype(F32)
                    part = pltpu.roll(part[cut[0] : cut[1]], 64, 1)
                    return part.reshape(tiles)

                pieces = [load(table[b, base], 384)]
                mid = table[b, base + 1]
                for j in range(4):
                    pieces.append(load(mid, 128 * j))
                pieces.append(load(table[b, base + 2], 0))
                for k in range(5):
                    asm[y_pos, dst[0] : dst[1], :, 128 * k : 128 * k + 128] = jnp.where(
                        low, pieces[k], pieces[k + 1]
                    )
        sub = lax.broadcasted_iota(jnp.int32, (10, 8, 128), 1)
        for k in range(5):
            at = slice(128 * k, 128 * k + 128)
            mid = asm[1, :, :, at]
            below = pltpu.roll(jnp.where(sub == 7, asm[0, :, :, at], mid), 1, 1)
            above = pltpu.roll(jnp.where(sub == 0, asm[2, :, :, at], mid), 7, 1)
            for dy, value in enumerate((below, mid, above)):
                split = value.reshape(5, 2, 8, 128)
                for dx in range(3):
                    tap = dx * 3 + dy
                    for ox in range(2):
                        start, parity = (dx + ox) // 2, (dx + ox) % 2
                        block = split[start : start + 4, parity].reshape(32, 128).astype(BF16)
                        for p, part in ((k, 0), (k - 1, 1)):
                            if 0 <= p < 4:
                                at_row = pl.multiple_of(ox * half_rows + b * 128 + p * 32, 32)
                                col = tap * 256 + part * 128
                                lhs[pl.ds(at_row, 32), col : col + 128] = block
        spread = keepx[b].astype(F32).reshape(4, 2, 8, 512)
        for ox in range(2):
            for p in range(4):
                at_row = pl.multiple_of(ox * half_rows + b * 128 + p * 32, 32)
                keep[pl.ds(at_row, 32), :] = spread[:, ox, :, 128 * p : 128 * p + 128].reshape(32, 128)
        return carry

    lax.fori_loop(0, count, gather_brick, 0)

    def forward(i, carry):
        at = pl.ds(pl.multiple_of(i * 256, 256), 256)
        value = jnp.dot(lhs[at, :], wpair[...], preferred_element_type=F32) * keep[at, :]
        pre[at, :] = value
        hid[at, :] = value * jax.nn.sigmoid(value)
        return carry

    lax.fori_loop(0, count, forward, 0)

    coarse_rows = count * 64
    child = []
    summed = None
    coarse = None
    for o in range(4):
        at = pl.ds((o // 2) * half_rows + o % 2, coarse_rows, stride=2)
        child.append(hid[at, :].astype(BF16))
        term = jnp.dot(child[o], down[o * 128 : o * 128 + 128, :], preferred_element_type=F32)
        summed = term if o == 0 else summed + term
        active = keep[at, :]
        coarse = active if o == 0 else jnp.maximum(coarse, active)
    coarse = jnp.maximum(coarse, pltpu.roll(coarse, 64, 1))
    sig = jax.nn.sigmoid(summed)
    result = (summed * sig * coarse).astype(BF16)
    cots = []
    for b in range(count):
        for p in range(4):
            lo = (b * 4 + p) * 16
            out[b, :, 128 * p : 128 * p + 128] = result[lo : lo + 16, :]
            cots.append(cot[b, :, 128 * p : 128 * p + 128])
    upstream = jnp.concatenate(cots, axis=0).astype(F32)
    grad_pre = (upstream * coarse * (sig * (1.0 + summed * (1.0 - sig)))).astype(BF16)
    for o in range(4):
        part = lax.dot_general(
            child[o], grad_pre, (((0,), (0,)), ((), ())), preferred_element_type=F32
        )
        wgrad[896 + o * 128 : 896 + o * 128 + 128, :] = part.astype(BF16)
        back = lax.dot_general(
            grad_pre,
            down[o * 128 : o * 128 + 128, :],
            (((1,), (1,)), ((), ())),
            preferred_element_type=F32,
        )
        hid[pl.ds((o // 2) * half_rows + o % 2, coarse_rows, stride=2), :] = back
    if wgrad.shape[0] > 1408:
        wgrad[1408:, :] = jnp.zeros((wgrad.shape[0] - 1408, 128), BF16)

    def hidden_grad(i, carry):
        at = pl.ds(pl.multiple_of(i * 256, 256), 256)
        value = hid[at, :] * silu_grad(pre[at, :]) * keep[at, :]
        grad[at, :] = value.astype(BF16)
        grad_t[:, at] = value.T.astype(BF16)
        return carry

    lax.fori_loop(0, count, hidden_grad, 0)

    wide = lax.broadcasted_iota(jnp.int32, (64, 128), 1)
    spare = None
    for tap in range(9):
        both = jnp.dot(
            grad_t[...], lhs[:, tap * 256 : tap * 256 + 256], preferred_element_type=F32
        )
        sums = both[0:64, :] + pltpu.roll(both[64:128, :], 192, 1)
        wgrad[tap * 64 : tap * 64 + 64, :] = sums[:, 0:128].astype(BF16)
        last = sums[:, 128:256]
        if tap % 2 == 0:
            spare = last
        if tap % 2 == 1 or tap == 8:
            other = pltpu.roll(last, 64, 1) if tap % 2 == 1 else jnp.zeros_like(last)
            lo = 576 + (tap // 2) * 64
            wgrad[lo : lo + 64, :] = jnp.where(wide < 64, spare, other).astype(BF16)

    def spread_brick(b, carry):
        low_rows = pl.multiple_of(b * 128, 128)
        for ox in range(2):
            dpad[ox * 128 : ox * 128 + 128, :] = lax.dot_general(
                grad[pl.ds(ox * half_rows + low_rows, 128), :],
                wpair[...],
                (((1,), (1,)), ((), ())),
                preferred_element_type=F32,
            )
        sub = lax.broadcasted_iota(jnp.int32, (8, 128), 0)
        for xp in range(10):
            for k in range(5):
                acc = [None, None, None]
                for dy in range(3):
                    for dx in range(3):
                        x = xp - dx
                        if not 0 <= x < 8:
                            continue
                        for p, part in ((k, 0), (k - 1, 1)):
                            if 0 <= p < 4:
                                at_row = (x % 2) * 128 + p * 32 + (x // 2) * 8
                                col = (dx * 3 + dy) * 256 + part * 128
                                tile = dpad[at_row : at_row + 8, col : col + 128]
                                acc[dy] = tile if acc[dy] is None else acc[dy] + tile
                below = pltpu.roll(acc[0], 7, 0)
                above = pltpu.roll(acc[2], 1, 0)
                mid = acc[1] + jnp.where(sub < 7, below, 0.0) + jnp.where(sub > 0, above, 0.0)
                at = slice(128 * k, 128 * k + 128)
                asm[0, xp, :, at] = pltpu.roll(jnp.where(sub == 7, below, 0.0), 64, 1)
                asm[1, xp, :, at] = pltpu.roll(mid, 64, 1)
                asm[2, xp, :, at] = pltpu.roll(jnp.where(sub == 0, above, 0.0), 64, 1)
        for x_pos in range(3):
            src = ((0, 1), (1, 9), (9, 10))[x_pos]
            dst = ((56, 64), (0, 64), (0, 8))[x_pos]
            size = dst[1] - dst[0]
            low = lax.broadcasted_iota(jnp.int32, (size, 128), 1) < 64
            for y_pos in range(3):
                base = x_pos * 9 + y_pos * 3
                tiles = [
                    asm[y_pos, src[0] : src[1], :, 128 * k : 128 * k + 128].reshape(size, 128)
                    for k in range(5)
                ]
                before, mid, after = table[b, base], table[b, base + 1], table[b, base + 2]
                here = slice(dst[0], dst[1])
                gext[before, here, 384:512] += jnp.where(low, 0.0, tiles[0])
                for j in range(4):
                    at = slice(128 * j, 128 * j + 128)
                    gext[mid, here, at] += jnp.where(low, tiles[j], tiles[j + 1])
                gext[after, here, 0:128] += jnp.where(low, tiles[4], 0.0)
        return carry

    lax.fori_loop(0, count, spread_brick, 0)

    def give_own(b, carry):
        own[b] = gext[b]
        return carry

    def give_back(s, carry):
        ret[s] = gext[count + s].astype(BF16)
        return carry

    lax.fori_loop(0, count, give_own, 0)
    lax.fori_loop(0, slots, give_back, 0)


def last_kernel(scale, chosen, own, came, keepx, wsum, grad_features, grad_conv, grad_down, acc):
    count = keepx.shape[0]
    slots = came.shape[0]
    for b in range(count):
        acc[b] = own[b]
    acc[count] = jnp.zeros((64, 512), F32)

    def add(s, carry):
        to = chosen[s]
        acc[to] = acc[to] + came[s].astype(F32)
        return carry

    lax.fori_loop(0, slots, add, 0)
    for b in range(count):
        grad_features[b] = (acc[b] * keepx[b].astype(F32)).astype(BF16)
    decode(scale, wsum, grad_conv, grad_down)


def decode(scale, wsum, grad_conv, grad_down):
    grad_down[...] = wsum[896:1408, :].astype(F32) * scale
    for tap in range(9):
        first = (wsum[tap * 64 : tap * 64 + 64, :].astype(F32) * scale).T
        grad_conv[tap * 192 : tap * 192 + 128, :] = first
    for pair in range(5):
        lo = 576 + pair * 64
        both = (wsum[lo : lo + 64, :].astype(F32) * scale).T
        for part in range(2):
            tap = 2 * pair + part
            if tap < 9:
                at = tap * 192 + 128
                grad_conv[at : at + 64, :] = both[part * 64 : part * 64 + 64, :]


def call(kernel, shapes, in_spaces, scratch, args):
    spaces = {"s": pltpu.SMEM, "v": pltpu.VMEM, "a": pl.ANY}
    return pl.pallas_call(
        kernel,
        out_shape=[jax.ShapeDtypeStruct(shape, kind) for shape, kind in shapes],
        in_specs=[pl.BlockSpec(memory_space=spaces[s]) for s in in_spaces],
        out_specs=[pl.BlockSpec(memory_space=pltpu.VMEM) for _ in shapes],
        scratch_shapes=scratch,
        compiler_params=pltpu.CompilerParams(vmem_limit_bytes=VMEM_BYTES),
    )(*args)


def shards(features, masks, rulebook, send_lists, conv_weight, down_weight, cotangent):
    count = features.shape[1]
    peers = lax.axis_size("spatial")
    devices = peers * lax.axis_size("dp")
    cap = send_lists.shape[3]
    slots = peers * cap
    total = count + slots + 1
    rows = count * 256
    unit = devices * 16
    wrows = -(-1408 // unit) * unit
    scale = float(devices * count * 512) ** (-0.5)
    chosen = send_lists.reshape(slots)
    brick = (64, 512)
    masked, keepx, outgoing = call(
        first_kernel,
        [((count + 1, *brick), BF16), ((count, *brick), BF16), ((slots, *brick), BF16)],
        "svv",
        [],
        (chosen, features.reshape(count, *brick), masks[0]),
    )
    arrived = lax.all_to_all(
        outgoing.reshape(peers, cap, *brick), "spatial", split_axis=0, concat_axis=0, tiled=True
    ).reshape(slots, *brick)
    out, own, ret, wgrad = call(
        main_kernel,
        [
            ((count, 16, 512), BF16),
            ((count, *brick), F32),
            ((slots, *brick), BF16),
            ((wrows, 128), BF16),
        ],
        "saavvvv",
        [
            pltpu.VMEM((total, *brick), BF16),
            pltpu.VMEM((total, *brick), F32),
            pltpu.VMEM((rows, 2304), BF16),
            pltpu.VMEM((3, 10, 8, 640), F32),
            pltpu.VMEM((256, 2304), F32),
            pltpu.VMEM((rows, 128), F32),
            pltpu.VMEM((rows, 128), F32),
            pltpu.VMEM((rows, 128), F32),
            pltpu.VMEM((rows, 128), BF16),
            pltpu.VMEM((128, rows), BF16),
            pltpu.VMEM((2304, 128), BF16),
            pltpu.SemaphoreType.DMA((2,)),
        ],
        (
            rulebook[0],
            masked,
            arrived,
            keepx,
            conv_weight.reshape(27 * 64, 64),
            down_weight.reshape(512, 128),
            cotangent.reshape(count, 16, 512),
        ),
    )
    came = lax.all_to_all(
        ret.reshape(peers, cap, *brick), "spatial", split_axis=0, concat_axis=0, tiled=True
    ).reshape(slots, *brick)
    parts = lax.all_to_all(
        wgrad.reshape(devices, wrows // devices, 128),
        ("spatial", "dp"),
        split_axis=0,
        concat_axis=0,
        tiled=True,
    )
    mine = parts.astype(F32).sum(axis=0).astype(BF16)
    wsum = lax.all_gather(mine, ("spatial", "dp"), axis=0, tiled=True)
    grad_features, grad_conv, grad_down = call(
        functools.partial(last_kernel, scale),
        [((count, *brick), BF16), ((27 * 64, 64), F32), ((512, 128), F32)],
        "svvvv",
        [pltpu.VMEM((count + 1, *brick), F32)],
        (chosen, own, came, keepx, wsum),
    )
    return (
        out.reshape(1, count, 4, 4, 512),
        grad_features.reshape(features.shape),
        grad_conv.reshape(27, 64, 64),
        grad_down.reshape(8, 64, 128),
    )


def solution(mesh):
    placed = (
        P("dp", "spatial", None, None, None),
        P("dp", "spatial", None),
        P("dp", "spatial", None),
        P("dp", "spatial", None, None),
        P(),
        P(),
        P("dp", "spatial", None, None, None),
    )
    return jax.shard_map(
        shards,
        mesh=mesh,
        in_specs=placed,
        out_specs=(
            P("dp", "spatial", None, None, None),
            P("dp", "spatial", None, None, None),
            P(),
            P(),
        ),
        check_vma=False,
    )
```

profile of v0, /device:TPU:0, one launch (start us, length us, event | category | flops | bytes accessed | tf_op | source)
XLA Modules:
  0.0 136.1 jit_solution(16132499216323991867)
XLA Ops:
  0.6 0.8 copy.12
  1.4 0.7 reshape.50.chosen
  2.0 1.3 copy.17
  3.4 3.1 %shard_map.102 = (bf16[7,64,512]{2,1,0:T(8,128)(2,1)}, bf16[6,64,512]{2,1,0:T(8,128)(2,1)}, bf16[16,64,512]{2,1,0:T(8,128)(2,1)}) custom-call(s32[16]{0:T(128)} %reshape.50.chosen, bf16[6,64,512]{2,1,0:T(8,128)(2,1)} %bitcast.24, s32[6,512]{1,0:T(8,128)} %bitcast.27), custom_call_target="tpu_custom_call" | custom-call | tf_op jit(solution)/shard_map/pallas_call | solution.py:298
  6.4 0.0 copy-start.4
  6.4 0.0 copy-start.2
  6.4 7.4 %all-to-all-start = ((bf16[8,2,64,512]{3,2,1,0:T(8,128)(2,1)}), bf16[8,2,64,512]{3,2,1,0:T(8,128)(2,1)S(1)}, u32[]{:S(2)}, u32[]{:S(2)}) async-start(bf16[8,2,64,512]{3,2,1,0:T(8,128)(2,1)} %bitcast.22), calls=%async_computation | async-start | bytes 2097152 | tf_op jit(solution)/shard_map/all_to_all | solution.py:328
  13.9 0.0 copy-done.4
  13.9 0.6 copy.18
  14.5 0.0 copy-done.2
  14.5 0.7 reshape.56.cot
  15.1 24.5 %all-to-all-done = bf16[8,2,64,512]{3,2,1,0:T(8,128)(2,1)S(1)} async-done(((bf16[8,2,64,512]{3,2,1,0:T(8,128)(2,1)}), bf16[8,2,64,512]{3,2,1,0:T(8,128)(2,1)S(1)}, u32[]{:S(2)}, u32[]{:S(2)}) %all-to-all-start) | async-done | bytes 1048608 | tf_op jit(solution)/shard_map/all_to_all | solution.py:328
  39.6 0.0 copy-start
  39.6 1.0 copy-done
  40.6 15.2 %shard_map.103 = (bf16[6,16,512]{2,1,0:T(8,128)(2,1)}, f32[6,64,512]{2,1,0:T(8,128)}, bf16[16,64,512]{2,1,0:T(8,128)(2,1)}, bf16[1536,128]{1,0:T(8,128)(2,1)}) custom-call(s32[6,27]{1,0:T(8,128)} %bitcast.28, bf16[7,64,512]{2,1,0:T(8,128)(2,1)} %get-tuple-element.14.masked, bf16[16,64,512]{2,1,0:T(8,128)(2,1)} %bitcast.19, ...), custom_call_target="tpu_custom_call" | custom-call | tf_op jit(solution)/shard_map/pallas_call | solution.py:298
  55.8 16.8 %all_to_all.15 = bf16[32,48,128]{2,1,0:T(8,128)(2,1)S(1)} all-to-all(bf16[32,48,128]{2,1,0:T(8,128)(2,1)} %bitcast.25), channel_id=1, replica_groups=mesh['spatial'=8,'dp'=4] {'spatial','dp'}, dimensions={0} | all-to-all | bytes 786432 | tf_op jit(solution)/shard_map/all_to_all | solution.py:367
  72.6 3.7 %all-to-all-start.1 = ((bf16[8,2,64,512]{3,2,1,0:T(8,128)(2,1)}), bf16[8,2,64,512]{3,2,1,0:T(8,128)(2,1)S(1)}, u32[]{:S(2)}, u32[]{:S(2)}) async-start(bf16[8,2,64,512]{3,2,1,0:T(8,128)(2,1)} %bitcast.21), calls=%async_computation.1 | async-start | bytes 2097152 | tf_op jit(solution)/shard_map/all_to_all | solution.py:364
  76.3 0.0 copy-done.3
  76.3 0.7 reshape.57
  77.0 0.1 reduce_sum.12
  77.1 54.6 %all_gather.3.wsum = bf16[1536,128]{1,0:T(8,128)(2,1)} all-gather(bf16[48,128]{1,0:T(8,128)(2,1)S(1)} %reduce_sum.12), channel_id=1, replica_groups=mesh['spatial'=8,'dp'=4] {'spatial','dp'}, dimensions={0}, use_global_device_ids=true | all-gather | bytes 405504 | tf_op jit(solution)/shard_map/all_gather | solution.py:375
  131.7 0.0 all-to-all-done.1
  131.7 1.0 copy-done.1
  132.7 3.4 %shard_map.104 = (bf16[6,64,512]{2,1,0:T(8,128)(2,1)}, f32[1728,64]{1,0:T(8,128)}, f32[512,128]{1,0:T(8,128)}) custom-call(s32[16]{0:T(128)} %reshape.50.chosen, f32[6,64,512]{2,1,0:T(8,128)} %get-tuple-element.18.own, bf16[16,64,512]{2,1,0:T(8,128)(2,1)} %bitcast.20, bf16[6,64,512]{2,1,0:T(8,128)(2,1)} %get-tuple-element.16.keepx, ...), custom_call_target="tpu_custom_call" | custom-call | tf_op jit(solution)/shard_map/pallas_call | solution.py:298
  (2 shorter events, 0.0 us)
Async XLA Ops:
  6.4 7.4 %copy-start.4 = (s32[1,6,27]{2,0,1:T(1,128)S(1)}, s32[1,6,27]{2,0,1:T(1,128)}, u32[]{:S(2)}) copy-start(s32[1,6,27]{2,0,1:T(1,128)} %param.9) | copy-start | bytes 1948
  6.4 8.0 %copy-start.2 = (bf16[1,6,4,4,512]{4,3,2,1,0:T(4,128)(2,1)S(1)}, bf16[1,6,4,4,512]{4,3,2,1,0:T(4,128)(2,1)}, u32[]{:S(2)}) copy-start(bf16[1,6,4,4,512]{4,3,2,1,0:T(4,128)(2,1)} %param.13) | copy-start | bytes 294916
  6.4 33.2 %all-to-all-start = ((bf16[8,2,64,512]{3,2,1,0:T(8,128)(2,1)}), bf16[8,2,64,512]{3,2,1,0:T(8,128)(2,1)S(1)}, u32[]{:S(2)}, u32[]{:S(2)}) async-start(bf16[8,2,64,512]{3,2,1,0:T(8,128)(2,1)} %bitcast.22), calls=%async_computation | async-start | bytes 2097152 | tf_op jit(solution)/shard_map/all_to_all | solution.py:328
  39.6 1.0 copy-start
  72.6 3.7 %copy-start.3 = (bf16[6,16,512]{2,1,0:T(8,128)(2,1)S(1)}, bf16[6,16,512]{2,1,0:T(8,128)(2,1)}, u32[]{:S(2)}) copy-start(bf16[6,16,512]{2,1,0:T(8,128)(2,1)} %get-tuple-element.17) | copy-start | bytes 294916
  72.6 59.1 %all-to-all-start.1 = ((bf16[8,2,64,512]{3,2,1,0:T(8,128)(2,1)}), bf16[8,2,64,512]{3,2,1,0:T(8,128)(2,1)S(1)}, u32[]{:S(2)}, u32[]{:S(2)}) async-start(bf16[8,2,64,512]{3,2,1,0:T(8,128)(2,1)} %bitcast.21), calls=%async_computation.1 | async-start | bytes 2097152 | tf_op jit(solution)/shard_map/all_to_all | solution.py:364
  131.7 1.0 copy-start.1
where the time goes:
time: 137 us; the launch traced here: 136 us
  blocking collectives  71.4 us (52%)
  waiting for transfers between devices  24.5 us (18%)
  Pallas kernels  21.6 us (16%)
  starting transfers between devices  11.1 us (8%)
  local copies, waits for them, and re-layouts  6.65 us (5%)
    all_gather x1, blocking collectives, shards(): wsum = lax.all_gather(mine, ('spatial', 'dp'), axis=0, tiled=True)  54.6 us
    all_to_all x1, waiting for transfers between devices, shards(): lax.all_to_all(outgoing.reshape(peers, cap, *brick), 'spatial', split_axi...  24.5 us
    pallas_call x3, Pallas kernels, call(): pl.pallas_call(kernel, out_shape=[jax.ShapeDtypeStruct(shape, kind) for s...  21.6 us
    all_to_all x1, blocking collectives, shards(): lax.all_to_all(wgrad.reshape(devices, wrows // devices, 128), ('spatial',...  16.8 us
    all_to_all x1, starting transfers between devices, shards(): lax.all_to_all(outgoing.reshape(peers, cap, *brick), 'spatial', split_axi...  7.41 us
    unnamed x13, local copies, waits for them, and re-layouts  4.66 us
    all_to_all x1, starting transfers between devices, shards(): lax.all_to_all(ret.reshape(peers, cap, *brick), 'spatial', split_axis=0,...  3.69 us
  transfers between devices with their start and end apart: 2, of which 1 were waited for; matrix products, arithmetic and copies ran while one was open for 1% of the time, Pallas kernels for 0%

commit v1 on v0

--- a/solution.py
+++ b/solution.py
@@ -260,6 +260,178 @@
     lax.fori_loop(0, slots, give_back, 0)
 
 
+def region(d, edge):
+    q = d // (edge * edge)
+    return (q % 2 * (edge // 2) + q // 2, d // edge % edge, d % edge)
+
+
+def relation(me, p, edge):
+    apart = [jnp.abs(a - b) for a, b in zip(region(me, edge), region(p, edge))]
+    near = jnp.maximum(jnp.maximum(apart[0], apart[1]), apart[2]) == 1
+    face = apart[0] + apart[1] + apart[2] == 1
+    return near, face
+
+
+def halo_copies(me, peers, source, landed, send_sem, recv_sem, act):
+    edge = round(peers ** (1 / 3))
+    for p in range(peers):
+        near, face = relation(me, p, edge)
+
+        def run(cap, p=p):
+            copy = pltpu.make_async_remote_copy(
+                src_ref=source.at[p, pl.ds(0, cap)],
+                dst_ref=landed.at[me, pl.ds(0, cap)],
+                send_sem=send_sem.at[p],
+                recv_sem=recv_sem.at[me],
+                device_id={"spatial": p},
+                device_id_type=pl.DeviceIdType.MESH,
+            )
+            back = pltpu.make_async_remote_copy(
+                src_ref=source.at[p, pl.ds(0, cap)],
+                dst_ref=landed.at[p, pl.ds(0, cap)],
+                send_sem=send_sem.at[p],
+                recv_sem=recv_sem.at[p],
+                device_id={"spatial": p},
+                device_id_type=pl.DeviceIdType.MESH,
+            )
+            act(copy, back)
+
+        @pl.when(near & face)
+        def _():
+            run(2)
+
+        @pl.when(near & jnp.logical_not(face))
+        def _():
+            run(1)
+
+
+def start_copy(copy, back):
+    copy.start()
+
+
+def end_copy(copy, back):
+    copy.wait_send()
+    back.wait_recv()
+
+
+def halo_kernel(peers, source, landed, send_sem, recv_sem):
+    me = lax.axis_index("spatial")
+    edge = round(peers ** (1 / 3))
+    barrier = pltpu.get_barrier_semaphore()
+    for p in range(peers):
+        near, _ = relation(me, p, edge)
+
+        @pl.when(near)
+        def _():
+            pl.semaphore_signal(
+                barrier, inc=1, device_id={"spatial": p}, device_id_type=pl.DeviceIdType.MESH
+            )
+
+    number = sum(relation(me, p, edge)[0].astype(jnp.int32) for p in range(peers))
+    pl.semaphore_wait(barrier, number)
+    halo_copies(me, peers, source, landed, send_sem, recv_sem, start_copy)
+    halo_copies(me, peers, source, landed, send_sem, recv_sem, end_copy)
+
+
+def back_kernel(
+    peers, groups, source, wgrad, landed, wsum,
+    send_sem, recv_sem, group_in, group_sum, peer_in, peer_sum, gathered,
+    gs_sem, gr_sem, ps_sem, pr_sem, as_sem, ar_sem, bs_sem, br_sem, own_sem,
+):
+    me = lax.axis_index("spatial")
+    mine = lax.axis_index("dp")
+    size = group_sum.shape[0]
+    unit = peer_sum.shape[0]
+    mesh = pl.DeviceIdType.MESH
+    barrier = pltpu.get_barrier_semaphore()
+    for k in range(1, peers):
+        pl.semaphore_signal(
+            barrier, inc=1, device_id={"spatial": (me + k) % peers}, device_id_type=mesh
+        )
+    for k in range(1, groups):
+        pl.semaphore_signal(
+            barrier, inc=1, device_id={"dp": (mine + k) % groups}, device_id_type=mesh
+        )
+    pl.semaphore_wait(barrier, peers + groups - 2)
+
+    def group_copy(k):
+        to = (mine + k) % groups
+        return pltpu.make_async_remote_copy(
+            src_ref=wgrad.at[pl.ds(to * size, size)],
+            dst_ref=group_in.at[k - 1],
+            send_sem=gs_sem.at[k - 1],
+            recv_sem=gr_sem.at[k - 1],
+            device_id={"dp": to},
+            device_id_type=mesh,
+        )
+
+    def peer_copy(k):
+        to = (me + k) % peers
+        return pltpu.make_async_remote_copy(
+            src_ref=group_sum.at[pl.ds(to * unit, unit)],
+            dst_ref=peer_in.at[k - 1],
+            send_sem=ps_sem.at[k - 1],
+            recv_sem=pr_sem.at[k - 1],
+            device_id={"spatial": to},
+            device_id_type=mesh,
+        )
+
+    def gather_copy(k, owner):
+        return pltpu.make_async_remote_copy(
+            src_ref=peer_sum,
+            dst_ref=gathered.at[pl.ds(owner * unit, unit)],
+            send_sem=as_sem.at[k - 1],
+            recv_sem=ar_sem.at[k - 1],
+            device_id={"spatial": (me + k) % peers},
+            device_id_type=mesh,
+        )
+
+    def spread_copy(k, owner):
+        return pltpu.make_async_remote_copy(
+            src_ref=gathered,
+            dst_ref=wsum.at[pl.ds(owner * size, size)],
+            send_sem=bs_sem.at[k - 1],
+            recv_sem=br_sem.at[k - 1],
+            device_id={"dp": (mine + k) % groups},
+            device_id_type=mesh,
+        )
+
+    for k in range(1, groups):
+        group_copy(k).start()
+    halo_copies(me, peers, source, landed, send_sem, recv_sem, start_copy)
+    total = wgrad[pl.ds(mine * size, size), :].astype(F32)
+    for k in range(1, groups):
+        group_copy(k).wait_recv()
+        total = total + group_in[k - 1].astype(F32)
+    group_sum[...] = total.astype(BF16)
+    for k in range(1, peers):
+        peer_copy(k).start()
+    part = group_sum[pl.ds(me * unit, unit), :].astype(F32)
+    for k in range(1, peers):
+        peer_copy(k).wait_recv()
+        part = part + peer_in[k - 1].astype(F32)
+    peer_sum[...] = part.astype(BF16)
+    for k in range(1, peers):
+        gather_copy(k, me).start()
+    gathered[pl.ds(me * unit, unit), :] = part.astype(BF16)
+    for k in range(1, peers):
+        gather_copy(k, (me + peers - k) % peers).wait_recv()
+    own = pltpu.make_async_copy(gathered, wsum.at[pl.ds(mine * size, size)], own_sem)
+    own.start()
+    for k in range(1, groups):
+        spread_copy(k, mine).start()
+    for k in range(1, groups):
+        spread_copy(k, (mine + groups - k) % groups).wait_recv()
+    own.wait()
+    for k in range(1, groups):
+        group_copy(k).wait_send()
+        spread_copy(k, mine).wait_send()
+    for k in range(1, peers):
+        peer_copy(k).wait_send()
+        gather_copy(k, me).wait_send()
+    halo_copies(me, peers, source, landed, send_sem, recv_sem, end_copy)
+
+
 def last_kernel(scale, chosen, own, came, keepx, wsum, grad_features, grad_conv, grad_down, acc):
     count = keepx.shape[0]
     slots = came.shape[0]
@@ -293,15 +465,18 @@
                 grad_conv[at : at + 64, :] = both[part * 64 : part * 64 + 64, :]
 
 
-def call(kernel, shapes, in_spaces, scratch, args):
+def call(kernel, shapes, in_spaces, scratch, args, collective=None):
+    remote = collective is not None
     spaces = {"s": pltpu.SMEM, "v": pltpu.VMEM, "a": pl.ANY}
     return pl.pallas_call(
         kernel,
         out_shape=[jax.ShapeDtypeStruct(shape, kind) for shape, kind in shapes],
         in_specs=[pl.BlockSpec(memory_space=spaces[s]) for s in in_spaces],
-        out_specs=[pl.BlockSpec(memory_space=pltpu.VMEM) for _ in shapes],
+        out_specs=[pl.BlockSpec(memory_space=pl.ANY if remote else pltpu.VMEM) for _ in shapes],
         scratch_shapes=scratch,
-        compiler_params=pltpu.CompilerParams(vmem_limit_bytes=VMEM_BYTES),
+        compiler_params=pltpu.CompilerParams(
+            vmem_limit_bytes=VMEM_BYTES, collective_id=collective, has_side_effects=remote
+        ),
     )(*args)
 
 
@@ -325,9 +500,16 @@
         [],
         (chosen, features.reshape(count, *brick), masks[0]),
     )
-    arrived = lax.all_to_all(
-        outgoing.reshape(peers, cap, *brick), "spatial", split_axis=0, concat_axis=0, tiled=True
-    ).reshape(slots, *brick)
+    sems = [pltpu.SemaphoreType.DMA((peers,)), pltpu.SemaphoreType.DMA((peers,))]
+    (arrived,) = call(
+        functools.partial(halo_kernel, peers),
+        [((peers, cap, *brick), BF16)],
+        "a",
+        sems,
+        (outgoing.reshape(peers, cap, *brick),),
+        collective=0,
+    )
+    arrived = arrived.reshape(slots, *brick)
     out, own, ret, wgrad = call(
         main_kernel,
         [
@@ -361,18 +543,29 @@
             cotangent.reshape(count, 16, 512),
         ),
     )
-    came = lax.all_to_all(
-        ret.reshape(peers, cap, *brick), "spatial", split_axis=0, concat_axis=0, tiled=True
-    ).reshape(slots, *brick)
-    parts = lax.all_to_all(
-        wgrad.reshape(devices, wrows // devices, 128),
-        ("spatial", "dp"),
-        split_axis=0,
-        concat_axis=0,
-        tiled=True,
-    )
-    mine = parts.astype(F32).sum(axis=0).astype(BF16)
-    wsum = lax.all_gather(mine, ("spatial", "dp"), axis=0, tiled=True)
+    groups = devices // peers
+    size = wrows // groups
+    unit = wrows // devices
+    came, wsum = call(
+        functools.partial(back_kernel, peers, groups),
+        [((peers, cap, *brick), BF16), ((wrows, 128), BF16)],
+        "av",
+        sems
+        + [
+            pltpu.VMEM((groups - 1, size, 128), BF16),
+            pltpu.VMEM((size, 128), BF16),
+            pltpu.VMEM((peers - 1, unit, 128), BF16),
+            pltpu.VMEM((unit, 128), BF16),
+            pltpu.VMEM((size, 128), BF16),
+        ]
+        + [pltpu.SemaphoreType.DMA((groups - 1,))] * 2
+        + [pltpu.SemaphoreType.DMA((peers - 1,))] * 4
+        + [pltpu.SemaphoreType.DMA((groups - 1,))] * 2
+        + [pltpu.SemaphoreType.DMA],
+        (ret.reshape(peers, cap, *brick), wgrad),
+        collective=1,
+    )
+    came = came.reshape(slots, *brick)
     grad_features, grad_conv, grad_down = call(
         functools.partial(last_kernel, scale),
         [((count, *brick), BF16), ((27 * 64, 64), F32), ((512, 128), F32)],

time: 137 us -> 81.1 us (0.59)
  blocking collectives: 71.4 us -> 0 us
  Pallas kernels: 21.6 us -> 73.3 us
  waiting for transfers between devices: 24.5 us -> 0 us
  starting transfers between devices: 11.1 us -> 0 us
    all_gather x1 -> x0, blocking collectives: 54.6 us -> none  [shards(): wsum = lax.all_gather(mine, ('spatial', 'dp'), axis=0, tiled=True)]
    pallas_call x3 -> x5, Pallas kernels: 21.6 us -> 73.3 us  [call(): pl.pallas_call(kernel, out_shape=[jax.ShapeDtypeStruct(shape, kind) for s...]
    all_to_all x2 -> x0, waiting for transfers between devices: 24.5 us -> none  [the longest x1 24.5 us: shards(): lax.all_to_all(outgoing.reshape(peers, cap, *brick), 'spatial', split_axi...]
    all_to_all x1 -> x0, blocking collectives: 16.8 us -> none  [shards(): lax.all_to_all(wgrad.reshape(devices, wrows // devices, 128), ('spatial',...]
    all_to_all x2 -> x0, starting transfers between devices: 11.1 us -> none  [the longest x1 7.41 us: shards(): lax.all_to_all(outgoing.reshape(peers, cap, *brick), 'spatial', split_axi...]
    unnamed x13 -> x7, local copies, waits for them, and re-layouts: 4.66 us -> 2.61 us
  transfers between devices with their start and end apart: 2 -> 0, of which waited for: 1 -> 0; matrix products, arithmetic and copies ran while one was open for 1% -> 0% of each run, Pallas kernels for 0% -> 0%
where the time goes in v1:
time: 81.1 us; the launch traced here: 80.3 us
  Pallas kernels  73.3 us (90%)
  local copies, waits for them, and re-layouts  6.29 us (8%)
    pallas_call x5, Pallas kernels, call(): pl.pallas_call(kernel, out_shape=[jax.ShapeDtypeStruct(shape, kind) for s...  73.3 us
    unnamed x7, local copies, waits for them, and re-layouts  2.61 us

profile of v1, /device:TPU:0, one launch (start us, length us, event | category | flops | bytes accessed | tf_op | source)
XLA Modules:
  0.0 80.3 jit_solution(16025267196458944563)
XLA Ops:
  0.6 0.0 copy-start.1
  0.6 0.0 copy-start
  0.7 0.7 copy-done.1
  1.3 0.6 copy.18
  1.9 0.8 copy.12
  2.6 0.6 reshape.47.chosen
  3.2 0.0 copy-done
  3.2 0.6 copy.17
  3.8 1.6 %reshape.53.cot = bf16[6,16,512]{2,1,0:T(8,128)(2,1)} reshape(bf16[1,6,4,4,512]{4,3,2,1,0:T(4,128)(2,1)} %param.13) | data formatting | bytes 196608 | tf_op jit(solution)/shard_map/reshape | solution.py:543
  5.4 3.1 %shard_map.102 = (bf16[7,64,512]{2,1,0:T(8,128)(2,1)}, bf16[6,64,512]{2,1,0:T(8,128)(2,1)}, bf16[16,64,512]{2,1,0:T(8,128)(2,1)}) custom-call(s32[16]{0:T(128)} %reshape.47.chosen, bf16[6,64,512]{2,1,0:T(8,128)(2,1)} %bitcast.23, s32[6,512]{1,0:T(8,128)} %bitcast.25), custom_call_target="tpu_custom_call" | custom-call | tf_op jit(solution)/shard_map/pallas_call | solution.py:471
  8.5 17.7 %shard_map.103 = bf16[8,2,64,512]{3,2,1,0:T(8,128)(2,1)} custom-call(bf16[8,2,64,512]{3,2,1,0:T(8,128)(2,1)} %bitcast.21), custom_call_target="tpu_custom_call" | custom-call | tf_op jit(solution)/shard_map/pallas_call | solution.py:471
  26.2 15.2 %shard_map.104 = (bf16[6,16,512]{2,1,0:T(8,128)(2,1)}, f32[6,64,512]{2,1,0:T(8,128)}, bf16[16,64,512]{2,1,0:T(8,128)(2,1)}, bf16[1536,128]{1,0:T(8,128)(2,1)}) custom-call(s32[6,27]{1,0:T(8,128)} %bitcast.26, bf16[7,64,512]{2,1,0:T(8,128)(2,1)} %get-tuple-element.16.masked, bf16[16,64,512]{2,1,0:T(8,128)(2,1)} %bitcast.18, ...), custom_call_target="tpu_custom_call" | custom-call | tf_op jit(solution)/shard_map/pallas_call | solution.py:471
  41.3 1.6 %reshape.54 = bf16[1,6,4,4,512]{4,3,2,1,0:T(4,128)(2,1)} reshape(bf16[6,16,512]{2,1,0:T(8,128)(2,1)} %get-tuple-element.19) | data formatting | bytes 196608 | tf_op jit(solution)/shard_map/reshape | solution.py:577
  42.9 34.0 %shard_map.105 = (bf16[8,2,64,512]{3,2,1,0:T(8,128)(2,1)}, bf16[1536,128]{1,0:T(8,128)(2,1)}) custom-call(bf16[8,2,64,512]{3,2,1,0:T(8,128)(2,1)} %bitcast.19, bf16[1536,128]{1,0:T(8,128)(2,1)} %get-tuple-element.22.wgrad), custom_call_target="tpu_custom_call" | custom-call | tf_op jit(solution)/shard_map/pallas_call | solution.py:471
  76.9 3.4 %shard_map.106 = (bf16[6,64,512]{2,1,0:T(8,128)(2,1)}, f32[1728,64]{1,0:T(8,128)}, f32[512,128]{1,0:T(8,128)}) custom-call(s32[16]{0:T(128)} %reshape.47.chosen, f32[6,64,512]{2,1,0:T(8,128)} %get-tuple-element.20.own, bf16[16,64,512]{2,1,0:T(8,128)(2,1)} %bitcast.20, bf16[6,64,512]{2,1,0:T(8,128)(2,1)} %get-tuple-element.18.keepx, ...), custom_call_target="tpu_custom_call" | custom-call | tf_op jit(solution)/shard_map/pallas_call | solution.py:471
Async XLA Ops:
  0.6 0.7 copy-start.1
  0.6 2.6 %copy-start = (s32[1,6,512]{2,0,1:T(1,128)S(1)}, s32[1,6,512]{2,0,1:T(1,128)}, u32[]{:S(2)}) copy-start(s32[1,6,512]{2,0,1:T(1,128)} %param.8) | copy-start | bytes 36868

commit v2 on v1

--- a/solution.py
+++ b/solution.py
@@ -17,7 +17,31 @@
     return sig * (1.0 + value * (1.0 - sig))
 
 
-def first_kernel(chosen, feats, mask, masked, keepx, outgoing):
+def pack(value, stage):
+    for k in range(4):
+        stage[k] = value[:, 128 * k : 128 * k + 128]
+    tiles = [stage[k, 0:8, :] for k in range(4)]
+    tiles += [stage[k, 56:64, :] for k in range(4)]
+    tiles += [stage[k, pl.ds(0, 8, stride=8), :] for k in range(4)]
+    tiles += [stage[k, pl.ds(7, 8, stride=8), :] for k in range(4)]
+    low = lax.broadcasted_iota(jnp.int32, (48, 128), 1) < 64
+    tiles.append(jnp.where(low, stage[0, 8:56, :], stage[3, 8:56, :]))
+    return jnp.concatenate(tiles, axis=0).astype(BF16)
+
+
+def unpack(rim, stage):
+    value = rim.astype(F32)
+    low = lax.broadcasted_iota(jnp.int32, (48, 128), 1) < 64
+    stage[0, 8:56, :] = jnp.where(low, value[128:176], 0.0)
+    stage[3, 8:56, :] = jnp.where(low, 0.0, value[128:176])
+    for k in range(4):
+        stage[k, pl.ds(0, 8, stride=8), :] = value[64 + 8 * k : 72 + 8 * k]
+        stage[k, pl.ds(7, 8, stride=8), :] = value[96 + 8 * k : 104 + 8 * k]
+        stage[k, 0:8, :] = value[8 * k : 8 * k + 8]
+        stage[k, 56:64, :] = value[32 + 8 * k : 40 + 8 * k]
+
+
+def first_kernel(chosen, feats, mask, masked, keepx, outgoing, work, rims):
     count = feats.shape[0]
     slots = outgoing.shape[0]
     vox = lax.broadcasted_iota(jnp.int32, (64, 512), 1)
@@ -30,11 +54,13 @@
         picked = jnp.where(own_row, mask[b : b + 1, :].astype(F32), 0.0).astype(BF16)
         keep = jnp.dot(picked, spread, preferred_element_type=F32)
         keepx[b] = keep.astype(BF16)
-        masked[b] = (feats[b].astype(F32) * keep).astype(BF16)
-    masked[count] = jnp.zeros((64, 512), BF16)
+        value = feats[b].astype(F32) * keep
+        masked[b] = value.astype(BF16)
+        rims[b] = pack(value, work.at[b])
+    rims[count] = jnp.zeros((176, 128), BF16)
 
     def send(s, carry):
-        outgoing[s] = masked[chosen[s]]
+        outgoing[s] = rims[chosen[s]]
         return carry
 
     lax.fori_loop(0, slots, send, 0)
@@ -43,7 +69,7 @@
 def main_kernel(
     table, masked, arrived, keepx, weight, down, cot,
     out, own, ret, wgrad,
-    ext, gext, lhs, asm, dpad, pre, hid, keep, grad, grad_t, wpair, sems,
+    ext, gext, lhs, asm, dpad, pre, hid, keep, grad, grad_t, wpair, work, sems,
 ):
     count = keepx.shape[0]
     slots = arrived.shape[0]
@@ -52,10 +78,17 @@
     rows = 2 * half_rows
     lane = lax.broadcasted_iota(jnp.int32, (8, 128), 1)
 
-    fetch_own = pltpu.make_async_copy(masked.at[pl.ds(0, count)], ext.at[pl.ds(0, count)], sems.at[0])
-    fetch_rest = pltpu.make_async_copy(arrived, ext.at[pl.ds(count, slots)], sems.at[1])
+    fetch_own = pltpu.make_async_copy(masked, ext.at[pl.ds(0, count)], sems.at[0])
     fetch_own.start()
-    fetch_rest.start()
+    work[...] = jnp.zeros((4, 64, 128), F32)
+
+    def put_arrived(s, carry):
+        unpack(arrived[s], work)
+        for k in range(4):
+            ext[count + s, :, 128 * k : 128 * k + 128] = work[k].astype(BF16)
+        return carry
+
+    lax.fori_loop(0, slots, put_arrived, 0)
     ext[total - 1] = jnp.zeros((64, 512), BF16)
 
     def clear(e, carry):
@@ -71,7 +104,6 @@
         right = jnp.concatenate([zero, taps], axis=0)
         wpair[tap * 256 : tap * 256 + 256, :] = jnp.concatenate([left, right], axis=1).astype(BF16)
     fetch_own.wait()
-    fetch_rest.wait()
 
     def gather_brick(b, carry):
         for y_pos in range(3):
@@ -253,7 +285,7 @@
         return carry
 
     def give_back(s, carry):
-        ret[s] = gext[count + s].astype(BF16)
+        ret[s] = pack(gext[count + s], work)
         return carry
 
     lax.fori_loop(0, count, give_own, 0)
@@ -272,7 +304,7 @@
     return near, face
 
 
-def halo_copies(me, peers, source, landed, send_sem, recv_sem, act):
+def halo_copies(me, peers, source, landed, send_sem, recv_sem, act, faces=True, others=True):
     edge = round(peers ** (1 / 3))
     for p in range(peers):
         near, face = relation(me, p, edge)
@@ -296,13 +328,17 @@
             )
             act(copy, back)
 
-        @pl.when(near & face)
-        def _():
-            run(2)
-
-        @pl.when(near & jnp.logical_not(face))
-        def _():
-            run(1)
+        if faces:
+
+            @pl.when(near & face)
+            def _():
+                run(2)
+
+        if others:
+
+            @pl.when(near & jnp.logical_not(face))
+            def _():
+                run(1)
 
 
 def start_copy(copy, back):
@@ -398,7 +434,7 @@
 
     for k in range(1, groups):
         group_copy(k).start()
-    halo_copies(me, peers, source, landed, send_sem, recv_sem, start_copy)
+    halo_copies(me, peers, source, landed, send_sem, recv_sem, start_copy, others=False)
     total = wgrad[pl.ds(mine * size, size), :].astype(F32)
     for k in range(1, groups):
         group_copy(k).wait_recv()
@@ -413,6 +449,7 @@
     peer_sum[...] = part.astype(BF16)
     for k in range(1, peers):
         gather_copy(k, me).start()
+    halo_copies(me, peers, source, landed, send_sem, recv_sem, start_copy, faces=False)
     gathered[pl.ds(me * unit, unit), :] = part.astype(BF16)
     for k in range(1, peers):
         gather_copy(k, (me + peers - k) % peers).wait_recv()
@@ -432,16 +469,19 @@
     halo_copies(me, peers, source, landed, send_sem, recv_sem, end_copy)
 
 
-def last_kernel(scale, chosen, own, came, keepx, wsum, grad_features, grad_conv, grad_down, acc):
+def last_kernel(scale, chosen, own, came, keepx, wsum, grad_features, grad_conv, grad_down, acc, work):
     count = keepx.shape[0]
     slots = came.shape[0]
     for b in range(count):
         acc[b] = own[b]
     acc[count] = jnp.zeros((64, 512), F32)
+    work[...] = jnp.zeros((4, 64, 128), F32)
 
     def add(s, carry):
         to = chosen[s]
-        acc[to] = acc[to] + came[s].astype(F32)
+        unpack(came[s], work)
+        for k in range(4):
+            acc[to, :, 128 * k : 128 * k + 128] += work[k]
         return carry
 
     lax.fori_loop(0, slots, add, 0)
@@ -493,32 +533,33 @@
     scale = float(devices * count * 512) ** (-0.5)
     chosen = send_lists.reshape(slots)
     brick = (64, 512)
+    rim = (176, 128)
     masked, keepx, outgoing = call(
         first_kernel,
-        [((count + 1, *brick), BF16), ((count, *brick), BF16), ((slots, *brick), BF16)],
+        [((count, *brick), BF16), ((count, *brick), BF16), ((slots, *rim), BF16)],
         "svv",
-        [],
+        [pltpu.VMEM((count, 4, 64, 128), F32), pltpu.VMEM((count + 1, *rim), BF16)],
         (chosen, features.reshape(count, *brick), masks[0]),
     )
     sems = [pltpu.SemaphoreType.DMA((peers,)), pltpu.SemaphoreType.DMA((peers,))]
     (arrived,) = call(
         functools.partial(halo_kernel, peers),
-        [((peers, cap, *brick), BF16)],
+        [((peers, cap, *rim), BF16)],
         "a",
         sems,
-        (outgoing.reshape(peers, cap, *brick),),
+        (outgoing.reshape(peers, cap, *rim),),
         collective=0,
     )
-    arrived = arrived.reshape(slots, *brick)
+    arrived = arrived.reshape(slots, *rim)
     out, own, ret, wgrad = call(
         main_kernel,
         [
             ((count, 16, 512), BF16),
             ((count, *brick), F32),
-            ((slots, *brick), BF16),
+            ((slots, *rim), BF16),
             ((wrows, 128), BF16),
         ],
-        "saavvvv",
+        "savvvvv",
         [
             pltpu.VMEM((total, *brick), BF16),
             pltpu.VMEM((total, *brick), F32),
@@ -531,7 +572,8 @@
             pltpu.VMEM((rows, 128), BF16),
             pltpu.VMEM((128, rows), BF16),
             pltpu.VMEM((2304, 128), BF16),
-            pltpu.SemaphoreType.DMA((2,)),
+            pltpu.VMEM((4, 64, 128), F32),
+            pltpu.SemaphoreType.DMA((1,)),
         ],
         (
             rulebook[0],
@@ -548,7 +590,7 @@
     unit = wrows // devices
     came, wsum = call(
         functools.partial(back_kernel, peers, groups),
-        [((peers, cap, *brick), BF16), ((wrows, 128), BF16)],
+        [((peers, cap, *rim), BF16), ((wrows, 128), BF16)],
         "av",
         sems
         + [
@@ -562,15 +604,15 @@
         + [pltpu.SemaphoreType.DMA((peers - 1,))] * 4
         + [pltpu.SemaphoreType.DMA((groups - 1,))] * 2
         + [pltpu.SemaphoreType.DMA],
-        (ret.reshape(peers, cap, *brick), wgrad),
+        (ret.reshape(peers, cap, *rim), wgrad),
         collective=1,
     )
-    came = came.reshape(slots, *brick)
+    came = came.reshape(slots, *rim)
     grad_features, grad_conv, grad_down = call(
         functools.partial(last_kernel, scale),
         [((count, *brick), BF16), ((27 * 64, 64), F32), ((512, 128), F32)],
         "svvvv",
-        [pltpu.VMEM((count + 1, *brick), F32)],
+        [pltpu.VMEM((count + 1, *brick), F32), pltpu.VMEM((4, 64, 128), F32)],
         (chosen, own, came, keepx, wsum),
     )
     return (

time: 81.1 us -> 68.9 us (0.85)
  Pallas kernels: 73.3 us -> 61.4 us
    pallas_call x5, Pallas kernels: 73.3 us -> 61.4 us  [call(): pl.pallas_call(kernel, out_shape=[jax.ShapeDtypeStruct(shape, kind) for s...]
where the time goes in v2:
time: 68.9 us; the launch traced here: 68.5 us
  Pallas kernels  61.4 us (89%)
  local copies, waits for them, and re-layouts  6.42 us (9%)
    pallas_call x5, Pallas kernels, call(): pl.pallas_call(kernel, out_shape=[jax.ShapeDtypeStruct(shape, kind) for s...  61.4 us
    unnamed x7, local copies, waits for them, and re-layouts  2.62 us
    reshape x1, local copies, waits for them, and re-layouts, shards(): out.reshape(1, count, 4, 4, 512)  1.56 us
    reshape x1, local copies, waits for them, and re-layouts, shards(): cotangent.reshape(count, 16, 512)  1.56 us

profile of v2, /device:TPU:0, one launch (start us, length us, event | category | flops | bytes accessed | tf_op | source)
XLA Modules:
  0.0 68.5 jit_solution(12706364782589225073)
XLA Ops:
  0.6 0.0 copy-start.1
  0.6 0.0 copy-start
  0.7 0.7 copy-done.1
  1.3 0.6 copy.18
  1.9 0.8 %copy.12 = s32[1,1,8,2]{3,2,1,0:T(8,128)S(1)} copy(s32[1,1,8,2]{2,3,1,0:T(2,128)} %param.10) | data formatting | bytes 128 | tf_op args[3]
  2.7 0.7 reshape.47.chosen
  3.3 0.0 copy-done
  3.3 0.6 copy.17
  3.9 1.6 %reshape.53.cot = bf16[6,16,512]{2,1,0:T(8,128)(2,1)} reshape(bf16[1,6,4,4,512]{4,3,2,1,0:T(4,128)(2,1)} %param.13) | data formatting | bytes 196608 | tf_op jit(solution)/shard_map/reshape | solution.py:585
  5.5 3.0 %shard_map.102 = (bf16[6,64,512]{2,1,0:T(8,128)(2,1)}, bf16[6,64,512]{2,1,0:T(8,128)(2,1)}, bf16[16,176,128]{2,1,0:T(8,128)(2,1)}) custom-call(s32[16]{0:T(128)} %reshape.47.chosen, bf16[6,64,512]{2,1,0:T(8,128)(2,1)} %bitcast.23, s32[6,512]{1,0:T(8,128)} %bitcast.25), custom_call_target="tpu_custom_call" | custom-call | tf_op jit(solution)/shard_map/pallas_call | solution.py:511
  8.5 14.3 %shard_map.103 = bf16[8,2,176,128]{3,2,1,0:T(8,128)(2,1)} custom-call(bf16[8,2,176,128]{3,2,1,0:T(8,128)(2,1)} %bitcast.21), custom_call_target="tpu_custom_call" | custom-call | tf_op jit(solution)/shard_map/pallas_call | solution.py:511
  22.8 15.1 %shard_map.104 = (bf16[6,16,512]{2,1,0:T(8,128)(2,1)}, f32[6,64,512]{2,1,0:T(8,128)}, bf16[16,176,128]{2,1,0:T(8,128)(2,1)}, bf16[1536,128]{1,0:T(8,128)(2,1)}) custom-call(s32[6,27]{1,0:T(8,128)} %bitcast.26, bf16[6,64,512]{2,1,0:T(8,128)(2,1)} %get-tuple-element.16.masked, bf16[16,176,128]{2,1,0:T(8,128)(2,1)} %bitcast.18, ...), custom_call_target="tpu_custom_call" | custom-call | tf_op jit(solution)/shard_map/pallas_call | solution.py:511
  38.0 1.6 %reshape.54 = bf16[1,6,4,4,512]{4,3,2,1,0:T(4,128)(2,1)} reshape(bf16[6,16,512]{2,1,0:T(8,128)(2,1)} %get-tuple-element.19) | data formatting | bytes 196608 | tf_op jit(solution)/shard_map/reshape | solution.py:619
  39.5 25.5 %shard_map.105 = (bf16[8,2,176,128]{3,2,1,0:T(8,128)(2,1)}, bf16[1536,128]{1,0:T(8,128)(2,1)}) custom-call(bf16[8,2,176,128]{3,2,1,0:T(8,128)(2,1)} %bitcast.20, bf16[1536,128]{1,0:T(8,128)(2,1)} %get-tuple-element.22.wgrad), custom_call_target="tpu_custom_call" | custom-call | tf_op jit(solution)/shard_map/pallas_call | solution.py:511
  65.1 3.5 %shard_map.106 = (bf16[6,64,512]{2,1,0:T(8,128)(2,1)}, f32[1728,64]{1,0:T(8,128)}, f32[512,128]{1,0:T(8,128)}) custom-call(s32[16]{0:T(128)} %reshape.47.chosen, f32[6,64,512]{2,1,0:T(8,128)} %get-tuple-element.20.own, bf16[16,176,128]{2,1,0:T(8,128)(2,1)} %bitcast.19, bf16[6,64,512]{2,1,0:T(8,128)(2,1)} %get-tuple-element.18.keepx, ...), custom_call_target="tpu_custom_call" | custom-call | tf_op jit(solution)/shard_map/pallas_call | solution.py:511
Async XLA Ops:
  0.6 0.7 copy-start.1
  0.6 2.7 %copy-start = (s32[1,6,512]{2,0,1:T(1,128)S(1)}, s32[1,6,512]{2,0,1:T(1,128)}, u32[]{:S(2)}) copy-start(s32[1,6,512]{2,0,1:T(1,128)} %param.8) | copy-start | bytes 36868

commit v3 on v2

--- a/solution.py
+++ b/solution.py
@@ -44,6 +44,7 @@
 def first_kernel(chosen, feats, mask, masked, keepx, outgoing, work, rims):
     count = feats.shape[0]
     slots = outgoing.shape[0]
+    cap = chosen.shape[0]
     vox = lax.broadcasted_iota(jnp.int32, (64, 512), 1)
     row = lax.broadcasted_iota(jnp.int32, (64, 512), 0)
     own_row = (vox // 8) == row
@@ -51,7 +52,7 @@
     l_index = lax.broadcasted_iota(jnp.int32, (512, 512), 1)
     spread = ((v_index % 8) == (l_index // 64)).astype(F32).astype(BF16)
     for b in range(count):
-        picked = jnp.where(own_row, mask[b : b + 1, :].astype(F32), 0.0).astype(BF16)
+        picked = jnp.where(own_row, mask[b].astype(F32), 0.0).astype(BF16)
         keep = jnp.dot(picked, spread, preferred_element_type=F32)
         keepx[b] = keep.astype(BF16)
         value = feats[b].astype(F32) * keep
@@ -60,7 +61,7 @@
     rims[count] = jnp.zeros((176, 128), BF16)
 
     def send(s, carry):
-        outgoing[s] = rims[chosen[s]]
+        outgoing[s] = rims[chosen[s % cap, s // cap]]
         return carry
 
     lax.fori_loop(0, slots, send, 0)
@@ -69,7 +70,7 @@
 def main_kernel(
     table, masked, arrived, keepx, weight, down, cot,
     out, own, ret, wgrad,
-    ext, gext, lhs, asm, dpad, pre, hid, keep, grad, grad_t, wpair, work, sems,
+    ext, gext, lhs, asm, dpad, pre, hid, keep, grad, grad_t, wpair, work, coarse_work, sems,
 ):
     count = keepx.shape[0]
     slots = arrived.shape[0]
@@ -120,11 +121,11 @@
                     part = pltpu.roll(part[cut[0] : cut[1]], 64, 1)
                     return part.reshape(tiles)
 
-                pieces = [load(table[b, base], 384)]
-                mid = table[b, base + 1]
+                pieces = [load(table[b, 0, base], 384)]
+                mid = table[b, 0, base + 1]
                 for j in range(4):
                     pieces.append(load(mid, 128 * j))
-                pieces.append(load(table[b, base + 2], 0))
+                pieces.append(load(table[b, 0, base + 2], 0))
                 for k in range(5):
                     asm[y_pos, dst[0] : dst[1], :, 128 * k : 128 * k + 128] = jnp.where(
                         low, pieces[k], pieces[k + 1]
@@ -178,14 +179,20 @@
         coarse = active if o == 0 else jnp.maximum(coarse, active)
     coarse = jnp.maximum(coarse, pltpu.roll(coarse, 64, 1))
     sig = jax.nn.sigmoid(summed)
-    result = (summed * sig * coarse).astype(BF16)
-    cots = []
+    coarse_work[...] = summed * sig * coarse
     for b in range(count):
         for p in range(4):
-            lo = (b * 4 + p) * 16
-            out[b, :, 128 * p : 128 * p + 128] = result[lo : lo + 16, :]
-            cots.append(cot[b, :, 128 * p : 128 * p + 128])
-    upstream = jnp.concatenate(cots, axis=0).astype(F32)
+            for x in range(4):
+                lo = (b * 4 + p) * 16 + x * 4
+                at = slice(128 * p, 128 * p + 128)
+                out[b * 4 + x, :, at] = coarse_work[lo : lo + 4, :].astype(BF16)
+    for b in range(count):
+        for p in range(4):
+            for x in range(4):
+                lo = (b * 4 + p) * 16 + x * 4
+                at = slice(128 * p, 128 * p + 128)
+                coarse_work[lo : lo + 4, :] = cot[b * 4 + x, :, at].astype(F32)
+    upstream = coarse_work[...]
     grad_pre = (upstream * coarse * (sig * (1.0 + summed * (1.0 - sig)))).astype(BF16)
     for o in range(4):
         part = lax.dot_general(
@@ -269,7 +276,7 @@
                     asm[y_pos, src[0] : src[1], :, 128 * k : 128 * k + 128].reshape(size, 128)
                     for k in range(5)
                 ]
-                before, mid, after = table[b, base], table[b, base + 1], table[b, base + 2]
+                before, mid, after = table[b, 0, base], table[b, 0, base + 1], table[b, 0, base + 2]
                 here = slice(dst[0], dst[1])
                 gext[before, here, 384:512] += jnp.where(low, 0.0, tiles[0])
                 for j in range(4):
@@ -472,13 +479,14 @@
 def last_kernel(scale, chosen, own, came, keepx, wsum, grad_features, grad_conv, grad_down, acc, work):
     count = keepx.shape[0]
     slots = came.shape[0]
+    cap = chosen.shape[0]
     for b in range(count):
         acc[b] = own[b]
     acc[count] = jnp.zeros((64, 512), F32)
     work[...] = jnp.zeros((4, 64, 128), F32)
 
     def add(s, carry):
-        to = chosen[s]
+        to = chosen[s % cap, s // cap]
         unpack(came[s], work)
         for k in range(4):
             acc[to, :, 128 * k : 128 * k + 128] += work[k]
@@ -531,7 +539,7 @@
     unit = devices * 16
     wrows = -(-1408 // unit) * unit
     scale = float(devices * count * 512) ** (-0.5)
-    chosen = send_lists.reshape(slots)
+    chosen = send_lists[0, 0].T
     brick = (64, 512)
     rim = (176, 128)
     masked, keepx, outgoing = call(
@@ -539,7 +547,7 @@
         [((count, *brick), BF16), ((count, *brick), BF16), ((slots, *rim), BF16)],
         "svv",
         [pltpu.VMEM((count, 4, 64, 128), F32), pltpu.VMEM((count + 1, *rim), BF16)],
-        (chosen, features.reshape(count, *brick), masks[0]),
+        (chosen, features.reshape(count, *brick), masks.reshape(count, 1, 512)),
     )
     sems = [pltpu.SemaphoreType.DMA((peers,)), pltpu.SemaphoreType.DMA((peers,))]
     (arrived,) = call(
@@ -554,7 +562,7 @@
     out, own, ret, wgrad = call(
         main_kernel,
         [
-            ((count, 16, 512), BF16),
+            ((count * 4, 4, 512), BF16),
             ((count, *brick), F32),
             ((slots, *rim), BF16),
             ((wrows, 128), BF16),
@@ -573,16 +581,17 @@
             pltpu.VMEM((128, rows), BF16),
             pltpu.VMEM((2304, 128), BF16),
             pltpu.VMEM((4, 64, 128), F32),
+            pltpu.VMEM((count * 64, 128), F32),
             pltpu.SemaphoreType.DMA((1,)),
         ],
         (
-            rulebook[0],
+            rulebook.reshape(count, 1, 27),
             masked,
             arrived,
             keepx,
             conv_weight.reshape(27 * 64, 64),
             down_weight.reshape(512, 128),
-            cotangent.reshape(count, 16, 512),
+            cotangent.reshape(count * 4, 4, 512),
         ),
     )
     groups = devices // peers

time: 68.9 us -> 62.6 us (0.909)
  local copies, waits for them, and re-layouts: 6.42 us -> 0 us
    reshape x3 -> x0, local copies, waits for them, and re-layouts: 3.8 us -> none  [the longest x1 1.56 us: shards(): out.reshape(1, count, 4, 4, 512)]
    unnamed x7 -> x0, local copies, waits for them, and re-layouts: 2.62 us -> none
where the time goes in v3:
time: 62.6 us; the launch traced here: 62.4 us
  Pallas kernels  61.7 us (99%)
  between operations  0.65 us (1%)
    pallas_call x5, Pallas kernels, call(): pl.pallas_call(kernel, out_shape=[jax.ShapeDtypeStruct(shape, kind) for s...  61.7 us

profile of v3, /device:TPU:0, one launch (start us, length us, event | category | flops | bytes accessed | tf_op | source)
XLA Modules:
  0.0 62.4 jit_solution(3386532544622917092)
XLA Ops:
  0.6 3.1 %shard_map.102 = (bf16[6,64,512]{2,1,0:T(8,128)(2,1)}, bf16[6,64,512]{2,1,0:T(8,128)(2,1)}, bf16[16,176,128]{2,1,0:T(8,128)(2,1)}) custom-call(s32[2,8]{1,0:T(2,128)} %bitcast.26, bf16[6,64,512]{2,1,0:T(8,128)(2,1)} %bitcast.22, s32[6,1,512]{2,1,0:T(1,128)} %bitcast.25), custom_call_target="tpu_custom_call" | custom-call | tf_op jit(solution)/shard_map/pallas_call | solution.py:519
  3.7 14.3 %shard_map.103 = bf16[8,2,176,128]{3,2,1,0:T(8,128)(2,1)} custom-call(bf16[8,2,176,128]{3,2,1,0:T(8,128)(2,1)} %bitcast.19), custom_call_target="tpu_custom_call" | custom-call | tf_op jit(solution)/shard_map/pallas_call | solution.py:519
  18.1 15.2 %shard_map.104 = (bf16[24,4,512]{2,1,0:T(4,128)(2,1)}, f32[6,64,512]{2,1,0:T(8,128)}, bf16[16,176,128]{2,1,0:T(8,128)(2,1)}, bf16[1536,128]{1,0:T(8,128)(2,1)}) custom-call(s32[6,1,27]{2,1,0:T(1,128)} %bitcast.28, bf16[6,64,512]{2,1,0:T(8,128)(2,1)} %get-tuple-element.16.masked, bf16[16,176,128]{2,1,0:T(8,128)(2,1)} %bitcast.17, ...), custom_call_target="tpu_custom_call" | custom-call | tf_op jit(solution)/shard_map/pallas_call | solution.py:519
  33.3 25.5 %shard_map.105 = (bf16[8,2,176,128]{3,2,1,0:T(8,128)(2,1)}, bf16[1536,128]{1,0:T(8,128)(2,1)}) custom-call(bf16[8,2,176,128]{3,2,1,0:T(8,128)(2,1)} %bitcast.18, bf16[1536,128]{1,0:T(8,128)(2,1)} %get-tuple-element.22.wgrad), custom_call_target="tpu_custom_call" | custom-call | tf_op jit(solution)/shard_map/pallas_call | solution.py:519
  58.8 3.5 %shard_map.106 = (bf16[6,64,512]{2,1,0:T(8,128)(2,1)}, f32[1728,64]{1,0:T(8,128)}, f32[512,128]{1,0:T(8,128)}) custom-call(s32[2,8]{1,0:T(2,128)} %bitcast.27, f32[6,64,512]{2,1,0:T(8,128)} %get-tuple-element.20.own, bf16[16,176,128]{2,1,0:T(8,128)(2,1)} %bitcast.20, bf16[6,64,512]{2,1,0:T(8,128)(2,1)} %get-tuple-element.18.keepx, ...), custom_call_target="tpu_custom_call" | custom-call | tf_op jit(solution)/shard_map/pallas_call | solution.py:519
